TPU v7x, 32 devices: a whole 2x2x4 slice. The times are simulated.
32 devices in a mesh: gx: 8 (over z, core), gy: 4 (over y, x).
Axes of the slice: x: 2, y: 2, z: 4, core: 2. Of those that a mesh axis runs over, the one named last changes fastest.
Arguments:
- electric: float32 [3, 512, 128, 128], P(None, 'gx', 'gy'), may hold values from -6 to 6
- magnetic: float32 [3, 512, 128, 128], P(None, 'gx', 'gy'), may hold values from -6 to 6
- material_ids: int32 [512, 128, 128], P('gx', 'gy'), may hold values from 0 to 7
- inv_permittivity: float32 [8], replicated, may hold values from 0.08 to 1
- forward_field: bfloat16 [3, 3, 512, 128, 128], P(None, None, 'gx', 'gy'), may hold values from -6 to 6
- source_values: float32 [16384, 384], P(('gx', 'gy')), may hold values from -6 to 6
- source_tile: int32 [16384, 1], P(('gx', 'gy')), may hold values from 0 to 31; in each aligned block of 512 rows (0 to 511, 512 to 1023, ...) at most 32 rows name the same one
- source_cell: int32 [16384], P(('gx', 'gy')), may hold values from 0 to 2047
- owner_map: int32 [16], replicated, may hold values from 0 to 31, as said below
- shape_basis: float32 [128, 64, 64], replicated, may hold values from -0.09375 to 0.09375
Outputs:
- adjoint_e: float32 [3, 512, 128, 128], P(None, 'gx', 'gy')
- adjoint_h: float32 [3, 512, 128, 128], P(None, 'gx', 'gy')
- design_gradient: float32 [32, 128], P(('gx', 'gy'))
Inputs may be any that keep to these rules, and one draw needn't show every extreme that they name: `source_tile`: each device's 512 source blocks name any one tile at most 32 times, a bound that some block reaches. `owner_map`: the owners of different design blocks are different devices; device 0 and the last device each own one.
All inputs are finite; a program needn't handle non-finite values.
Results may differ from a plain program's by a relative error of at most 0.0003.
Values sent between devices are 32-bit elements; how exact they have to be, the bound alone decides.
A program may use at most 128 MiB of HBM per device.

v0:
```python
import functools

import jax
import jax.numpy as jnp
from jax import lax
from jax.experimental import pallas as pl
from jax.experimental.pallas import tpu as pltpu
from jax.sharding import PartitionSpec as P

time_step = 0.5
corr_scale = 0.0625
PLANES = 4
MESH = pl.DeviceIdType.MESH


def split_bf16(value):
    high = value.astype(jnp.bfloat16)
    low = (value - high.astype(jnp.float32)).astype(jnp.bfloat16)
    return high, low


def kernel(
    grid_x,
    grid_y,
    tile_col,
    tile_row,
    cell_row,
    table,
    owners,
    values_hbm,
    electric_hbm,
    magnetic_hbm,
    ids_hbm,
    forward_hbm,
    basis_hbm,
    electric_out,
    magnetic_out,
    grad_out,
    values,
    e,
    h,
    ids,
    forward,
    basis,
    half_eps,
    acc,
    drive,
    one_hot,
    pack_hot,
    packed,
    got,
    cells_out,
    cells_got,
    cell_rows,
    halves,
    ex_out,
    ey_out,
    hx_out,
    hy_out,
    ex_in,
    ey_in,
    hx_in,
    hy_in,
    grad_send,
    grad_got,
    load_sem,
    store_sem,
    bulk_send,
    bulk_recv,
    halo_send,
    halo_recv,
):
    n = grid_x * grid_y
    width_x, width_y, depth = ids.shape
    steps = forward.shape[0]
    count = values.shape[0]
    rows = packed.shape[1]
    cap = rows // n
    per_lane = 128 // cap
    cell_total = width_x * width_y
    index_x = lax.axis_index("gx")
    index_y = lax.axis_index("gy")
    me = index_x * grid_y + index_y

    def place(device):
        return (device // grid_y, lax.rem(device, grid_y))

    def others(body):
        def step(k, carry):
            body(lax.rem(me + k, n))
            return carry

        lax.fori_loop(1, n, step, 0)

    barrier = pltpu.get_barrier_semaphore()

    def greet(device):
        pl.semaphore_signal(barrier, inc=1, device_id=place(device), device_id_type=MESH)

    others(greet)

    e_own = e.at[:, pl.ds(0, width_x)]
    h_own = h.at[:, pl.ds(1, width_x)]
    loads = [
        pltpu.make_async_copy(source, dest, load_sem.at[i])
        for i, (source, dest) in enumerate(
            [
                (values_hbm, values),
                (electric_hbm, e_own),
                (magnetic_hbm, h_own),
                (ids_hbm, ids),
                (forward_hbm, forward),
                (basis_hbm, basis),
            ]
        )
    ]
    for load in loads:
        load.start()

    trow = tile_row[...]
    same = (tile_col[...] == trow) & (
        lax.broadcasted_iota(jnp.int32, (count, count), 0)
        < lax.broadcasted_iota(jnp.int32, (count, count), 1)
    )
    slot = jnp.sum(jnp.where(same, 1.0, 0.0), axis=0, keepdims=True).astype(jnp.int32)
    dest = trow * cap + slot
    chunk = min(256, rows)

    def fill_pack(i, carry):
        start = pl.multiple_of(i * chunk, chunk)
        row = start + lax.broadcasted_iota(jnp.int32, (chunk, count), 0)
        pack_hot[pl.ds(start, chunk), :] = jnp.where(row == dest, 1.0, 0.0).astype(jnp.bfloat16)
        return carry

    lax.fori_loop(0, rows // chunk, fill_pack, 0)

    cell = cell_row[...] + 1
    lane_slot = slot + lax.rem(me, per_lane) * cap
    slot_hot = jnp.where(
        lax.broadcasted_iota(jnp.int32, (128, count), 0) == lane_slot, 1.0, 0.0
    ).astype(jnp.bfloat16)
    for_tile = lax.broadcasted_iota(jnp.int32, (n * 8, count), 0) // 8 == trow
    cell_high = jnp.where(for_tile, (cell // 64).astype(jnp.float32), 0.0).astype(jnp.bfloat16)
    cell_low = jnp.where(for_tile, lax.rem(cell, 64).astype(jnp.float32), 0.0).astype(jnp.bfloat16)
    lanes = (((1,), (1,)), ((), ()))
    sent_cells = 64.0 * lax.dot_general(
        cell_high, slot_hot, lanes, preferred_element_type=jnp.float32
    ) + lax.dot_general(cell_low, slot_hot, lanes, preferred_element_type=jnp.float32)
    cells_out[...] = sent_cells.reshape(n, 8, 128)
    cells_got[me] = cells_out[me]

    loads[0].wait()

    def pack(step):
        high, low = split_bf16(values[:, step * depth : (step + 1) * depth])
        both = jnp.concatenate([high, low], axis=1)

        def body(i, carry):
            start = pl.multiple_of(i * chunk, chunk)
            part = jnp.dot(
                pack_hot[pl.ds(start, chunk), :], both, preferred_element_type=jnp.float32
            )
            packed[step, pl.ds(start, chunk), :] = part[:, :depth] + part[:, depth:]
            return carry

        lax.fori_loop(0, rows // chunk, body, 0)
        mine = pl.ds(pl.multiple_of(me * cap, cap), cap)
        got[step, mine, :] = packed[step, mine, :]

    def send_values(step):
        mine = pl.ds(pl.multiple_of(me * cap, cap), cap)

        def send(device):
            pltpu.make_async_remote_copy(
                src_ref=packed.at[step, pl.ds(pl.multiple_of(device * cap, cap), cap)],
                dst_ref=got.at[step, mine],
                send_sem=bulk_send.at[step],
                recv_sem=bulk_recv.at[step],
                device_id=place(device),
                device_id_type=MESH,
            ).start()

        others(send)

    def wait_values(step, sem):
        part = got.at[step, pl.ds(0, (n - 1) * cap)]
        pltpu.make_async_copy(part, part, sem.at[step]).wait()

    def send_blocks(source, target, number):
        def send(device):
            pltpu.make_async_remote_copy(
                src_ref=source(device),
                dst_ref=target.at[me],
                send_sem=bulk_send.at[number],
                recv_sem=bulk_recv.at[number],
                device_id=place(device),
                device_id_type=MESH,
            ).start()

        others(send)

    def wait_blocks(target, sem, number):
        part = target.at[pl.ds(0, n - 1)]
        pltpu.make_async_copy(part, part, sem.at[number]).wait()

    pack(0)

    first_x = index_x == 0
    last_x = index_x == grid_x - 1
    first_y = index_y == 0
    last_y = index_y == grid_y - 1

    @pl.when(last_x)
    def _():
        ex_in[...] = jnp.zeros_like(ex_in)

    @pl.when(last_y)
    def _():
        ey_in[...] = jnp.zeros_like(ey_in)

    @pl.when(first_x)
    def _():
        hx_in[...] = jnp.zeros_like(hx_in)

    @pl.when(first_y)
    def _():
        hy_in[...] = jnp.zeros_like(hy_in)

    def halo(number, step, source, target, device):
        return pltpu.make_async_remote_copy(
            src_ref=source.at[step],
            dst_ref=target.at[step],
            send_sem=halo_send.at[number, step],
            recv_sem=halo_recv.at[number, step],
            device_id=device,
            device_id_type=MESH,
        )

    down_x = (jnp.maximum(index_x - 1, 0), index_y)
    up_x = (jnp.minimum(index_x + 1, grid_x - 1), index_y)
    down_y = (index_x, jnp.maximum(index_y - 1, 0))
    up_y = (index_x, jnp.minimum(index_y + 1, grid_y - 1))
    halos = [
        (0, ex_out, ex_in, down_x, ~first_x, ~last_x),
        (1, ey_out, ey_in, down_y, ~first_y, ~last_y),
        (2, hx_out, hx_in, up_x, ~last_x, ~first_x),
        (3, hy_out, hy_in, up_y, ~last_y, ~first_y),
    ]

    def halo_start(which, step):
        number, source, target, device, sends, _ = halos[which]

        @pl.when(sends)
        def _():
            halo(number, step, source, target, device).start()

    def halo_arrived(which, step):
        number, source, target, device, _, receives = halos[which]

        @pl.when(receives)
        def _():
            halo(number, step, source, target, device).wait_recv()

    def halo_left(which, step):
        number, source, target, device, sends, _ = halos[which]

        @pl.when(sends)
        def _():
            halo(number, step, source, target, device).wait_send()

    loads[1].wait()

    def stage_e(i, carry):
        for k in range(PLANES):
            x = i * PLANES + k
            ey_out[0, 0, pl.ds(x, 1), :] = e[0, x, pl.ds(0, 1), :]
            ey_out[0, 1, pl.ds(x, 1), :] = e[2, x, pl.ds(0, 1), :]
        return carry

    lax.fori_loop(0, width_x // PLANES, stage_e, 0)
    ex_out[0] = e[1:3, 0]

    pl.semaphore_wait(barrier, n - 1)
    halo_start(0, 0)
    halo_start(1, 0)
    send_blocks(lambda device: cells_out.at[device], cells_got, steps)
    send_values(0)
    for step in range(1, steps):
        pack(step)

    loads[3].wait()
    scalars = [time_step * table[m] for m in range(table.shape[0])]

    def fill_eps(i, carry):
        part = pl.ds(i * PLANES, PLANES)
        which = ids[part]
        value = jnp.zeros(which.shape, jnp.float32)
        for m, scalar in enumerate(scalars):
            value = jnp.where(which == m, scalar, value)
        half_eps[part] = value
        acc[part] = jnp.zeros(which.shape, jnp.float32)
        return carry

    lax.fori_loop(0, width_x // PLANES, fill_eps, 0)

    plane = (width_y, depth)
    row_id = lax.broadcasted_iota(jnp.int32, plane, 0)
    lane_id = lax.broadcasted_iota(jnp.int32, plane, 1)
    row_last, row_first = row_id == width_y - 1, row_id == 0
    lane_last, lane_first = lane_id == depth - 1, lane_id == 0

    def next_y(v, edge):
        return jnp.where(row_last, edge, pltpu.roll(v, width_y - 1, 0))

    def prev_y(v, edge):
        return jnp.where(row_first, edge, pltpu.roll(v, 1, 0))

    def next_z(v):
        return jnp.where(lane_last, 0.0, pltpu.roll(v, depth - 1, 1))

    def prev_z(v):
        return jnp.where(lane_first, 0.0, pltpu.roll(v, 1, 1))

    def h_phase(step):
        halo_arrived(0, step)
        e[1:3, width_x] = ex_in[step]
        halo_arrived(1, step)

        def body(i, carry):
            done = []
            for k in range(PLANES):
                x = i * PLANES + k
                ex, ey, ez = e[0, x], e[1, x], e[2, x]
                ey_next, ez_next = e[1, x + 1], e[2, x + 1]
                ex_y = next_y(ex, ey_in[step, 0, pl.ds(x, 1), :])
                ez_y = next_y(ez, ey_in[step, 1, pl.ds(x, 1), :])
                curl_x = (ez_y - ez) - (next_z(ey) - ey)
                curl_y = (next_z(ex) - ex) - (ez_next - ez)
                curl_z = (ey_next - ey) - (ex_y - ex)
                done.append(
                    (
                        x,
                        h[0, x + 1] - time_step * curl_x,
                        h[1, x + 1] - time_step * curl_y,
                        h[2, x + 1] - time_step * curl_z,
                    )
                )
            for x, hx, hy, hz in done:
                h[0, x + 1] = hx
                h[1, x + 1] = hy
                h[2, x + 1] = hz
                hy_out[step, 0, pl.ds(x, 1), :] = hx[width_y - 1 :, :]
                hy_out[step, 1, pl.ds(x, 1), :] = hz[width_y - 1 :, :]
            return carry

        lax.fori_loop(0, width_x // PLANES, body, 0)
        hx_out[step] = h[1:3, width_x]
        halo_start(2, step)
        halo_start(3, step)

    def e_phase(step, first, last):
        def body(i, carry):
            done = []
            for k in range(PLANES):
                x = i * PLANES + k
                hx, hy, hz = h[0, x + 1], h[1, x + 1], h[2, x + 1]
                hy_prev, hz_prev = h[1, x], h[2, x]
                hx_y = prev_y(hx, hy_in[step, 0, pl.ds(x, 1), :])
                hz_y = prev_y(hz, hy_in[step, 1, pl.ds(x, 1), :])
                back_x = (hz - hz_y) - (hy - prev_z(hy))
                back_y = (hx - prev_z(hx)) - (hz - hz_prev)
                back_z = (hy - hy_prev) - (hx - hx_y) - drive[x]
                scale = half_eps[x]
                ex = e[0, x] + scale * back_x
                ey = e[1, x] + scale * back_y
                ez = e[2, x] + scale * back_z
                total = (
                    acc[x]
                    + forward[step, 0, x].astype(jnp.float32) * ex
                    + forward[step, 1, x].astype(jnp.float32) * ey
                    + forward[step, 2, x].astype(jnp.float32) * ez
                )
                done.append((x, ex, ey, ez, total))
            for x, ex, ey, ez, total in done:
                e[0, x] = ex
                e[1, x] = ey
                e[2, x] = ez
                acc[x] = total
                if step + 1 < steps:
                    ey_out[step + 1, 0, pl.ds(x, 1), :] = ex[:1, :]
                    ey_out[step + 1, 1, pl.ds(x, 1), :] = ez[:1, :]
            return carry

        lax.fori_loop(first // PLANES, last // PLANES, body, 0)

    tile_rows = min(256, cell_total)

    def make_drive(step):
        high, low = split_bf16(got[step])
        halves[:, :depth] = high
        halves[:, depth:] = low

        def body(i, carry):
            start = pl.multiple_of(i * tile_rows, tile_rows)
            part = jnp.dot(
                one_hot[pl.ds(start, tile_rows), :],
                halves[...],
                preferred_element_type=jnp.float32,
            )
            drive[pl.ds(i * (tile_rows // width_y), tile_rows // width_y)] = (
                part[:, :depth] + part[:, depth:]
            ).reshape(tile_rows // width_y, width_y, depth)
            return carry

        lax.fori_loop(0, cell_total // tile_rows, body, 0)

    loads[2].wait()
    stores = []
    for step in range(steps):
        h_phase(step)
        if step == 0:
            loads[4].wait()
            loads[5].wait()
        if step + 1 < steps:
            send_values(step + 1)
        else:
            store = pltpu.make_async_copy(h_own, magnetic_out, store_sem.at[0])
            store.start()
            stores.append(store)
        if step == 0:
            wait_blocks(cells_got, bulk_recv, steps)
            for group in range(rows // 128):
                total = cells_got[group * per_lane]
                for k in range(1, per_lane):
                    total = total + cells_got[group * per_lane + k]
                cell_rows[group] = total.astype(jnp.int32) - 1

            def fill_hot(i, carry):
                start = pl.multiple_of(i * tile_rows, tile_rows)
                cell_id = start + lax.broadcasted_iota(jnp.int32, (tile_rows, 128), 0)
                for group in range(rows // 128):
                    hit = cell_id == cell_rows[group, 0:1, :]
                    one_hot[pl.ds(start, tile_rows), group * 128 : (group + 1) * 128] = (
                        jnp.where(hit, 1.0, 0.0).astype(jnp.bfloat16)
                    )
                return carry

            lax.fori_loop(0, cell_total // tile_rows, fill_hot, 0)
        wait_values(step, bulk_recv)
        make_drive(step)
        halo_arrived(2, step)
        h_store_plane = hx_in[step]
        h[1:3, 0] = h_store_plane
        halo_arrived(3, step)
        if step + 1 < steps:
            e_phase(step, 0, width_x)
            ex_out[step + 1] = e[1:3, 0]
            halo_start(0, step + 1)
            halo_start(1, step + 1)
        else:
            parts = 4
            size = width_x // parts
            for part in range(parts):
                e_phase(step, part * size, (part + 1) * size)
                store = pltpu.make_async_copy(
                    e.at[:, pl.ds(part * size, size)],
                    electric_out.at[:, pl.ds(part * size, size)],
                    store_sem.at[1 + part],
                )
                store.start()
                stores.append(store)

    side = basis.shape[1]
    offset = lax.rem(index_y * width_y, side)
    at_lane = lax.broadcasted_iota(jnp.int32, (width_y, side), 1) == (
        lax.broadcasted_iota(jnp.int32, (width_y, side), 0) + offset
    )
    column = jnp.sum(acc[...], axis=2, keepdims=True) * corr_scale
    corr = jnp.sum(jnp.where(at_lane[None], column, 0.0), axis=1)
    params = basis.shape[0]
    group = 16
    pieces = []
    ones = jnp.ones((8, side), jnp.float32)
    for start in range(0, params, group):
        pieces.append(jnp.sum(basis[start : start + group] * corr[None], axis=1))
    weighted = jnp.concatenate(pieces, axis=0)
    grad_send[...] = lax.dot_general(
        ones,
        weighted,
        (((1,), (1,)), ((), ())),
        preferred_element_type=jnp.float32,
        precision=lax.Precision.HIGHEST,
    )
    grad_got[me] = grad_send[...]
    send_blocks(lambda device: grad_send, grad_got, steps + 1)
    wait_blocks(grad_got, bulk_recv, steps + 1)

    def add(source, total):
        x, y = source // grid_y, lax.rem(source, grid_y)
        block = (x * width_x // side) * (width_y * grid_y // side) + y * width_y // side
        return total + jnp.where(owners[block] == me, grad_got[source], 0.0)

    total = lax.fori_loop(0, n, add, jnp.zeros(grad_send.shape, jnp.float32))
    grad_out[...] = total[:1, :]

    for store in stores:
        store.wait()
    for step in range(steps):
        wait_values(step, bulk_send)
        for which in range(4):
            halo_left(which, step)
    wait_blocks(cells_got, bulk_send, steps)
    wait_blocks(grad_got, bulk_send, steps + 1)


def per_device(
    electric,
    magnetic,
    material_ids,
    inv_permittivity,
    forward_field,
    source_values,
    source_tile,
    source_cell,
    owner_map,
    shape_basis,
):
    _, width_x, width_y, depth = electric.shape
    steps = forward_field.shape[0]
    grid_x = lax.axis_size("gx")
    grid_y = lax.axis_size("gy")
    n = grid_x * grid_y
    count = source_tile.shape[0]
    cap = max(2, 2 * count // n)
    rows = n * cap
    params = shape_basis.shape[0]
    f32, bf16 = jnp.float32, jnp.bfloat16
    vmem = pl.BlockSpec(memory_space=pltpu.VMEM)
    smem = pl.BlockSpec(memory_space=pltpu.SMEM)
    hbm = pl.BlockSpec(memory_space=pl.ANY)
    x_face = pltpu.VMEM((steps, 2, width_y, depth), f32)
    y_face = pltpu.VMEM((steps, 2, width_x, depth), f32)
    return pl.pallas_call(
        functools.partial(kernel, grid_x, grid_y),
        out_shape=(
            jax.ShapeDtypeStruct(electric.shape, f32),
            jax.ShapeDtypeStruct(magnetic.shape, f32),
            jax.ShapeDtypeStruct((1, params), f32),
        ),
        in_specs=[vmem, vmem, vmem, smem, smem] + [hbm] * 6,
        out_specs=(hbm, hbm, vmem),
        scratch_shapes=[
            pltpu.VMEM(source_values.shape, f32),
            pltpu.VMEM((3, width_x + 1, width_y, depth), f32),
            pltpu.VMEM((3, width_x + 1, width_y, depth), f32),
            pltpu.VMEM(material_ids.shape, jnp.int32),
            pltpu.VMEM(forward_field.shape, bf16),
            pltpu.VMEM(shape_basis.shape, f32),
            pltpu.VMEM(material_ids.shape, f32),
            pltpu.VMEM(material_ids.shape, f32),
            pltpu.VMEM(material_ids.shape, f32),
            pltpu.VMEM((width_x * width_y, rows), bf16),
            pltpu.VMEM((rows, count), bf16),
            pltpu.VMEM((steps, rows, depth), f32),
            pltpu.VMEM((steps, rows, depth), f32),
            pltpu.VMEM((n, 8, 128), f32),
            pltpu.VMEM((n, 8, 128), f32),
            pltpu.VMEM((rows // 128, 8, 128), jnp.int32),
            pltpu.VMEM((rows, 2 * depth), bf16),
            x_face,
            y_face,
            x_face,
            y_face,
            x_face,
            y_face,
            x_face,
            y_face,
            pltpu.VMEM((8, params), f32),
            pltpu.VMEM((n, 8, params), f32),
            pltpu.SemaphoreType.DMA((6,)),
            pltpu.SemaphoreType.DMA((5,)),
            pltpu.SemaphoreType.DMA((steps + 2,)),
            pltpu.SemaphoreType.DMA((steps + 2,)),
            pltpu.SemaphoreType.DMA((4, steps)),
            pltpu.SemaphoreType.DMA((4, steps)),
        ],
        compiler_params=pltpu.CompilerParams(
            collective_id=0, has_side_effects=True, vmem_limit_bytes=50 * 1024 * 1024
        ),
    )(
        source_tile,
        source_tile.reshape(1, count),
        source_cell.reshape(1, count),
        inv_permittivity,
        owner_map,
        source_values,
        electric,
        magnetic,
        material_ids,
        forward_field,
        shape_basis,
    )


def solution(mesh):
    placed = (
        P(None, "gx", "gy", None),
        P(None, "gx", "gy", None),
        P("gx", "gy", None),
        P(),
        P(None, None, "gx", "gy", None),
        P(("gx", "gy"), None),
        P(("gx", "gy"), None),
        P(("gx", "gy")),
        P(),
        P(),
    )
    return jax.shard_map(
        per_device,
        mesh=mesh,
        in_specs=placed,
        out_specs=(P(None, "gx", "gy", None), P(None, "gx", "gy", None), P(("gx", "gy"), None)),
        check_vma=False,
    )
```

profile of v0, /device:TPU:0, one launch (start us, length us, event | category | flops | bytes accessed | tf_op | source)
XLA Modules:
  0.0 78.5 jit_solution(15416137867963047648)
XLA Ops:
  0.6 0.8 %copy.13.tile_col = s32[512,1]{1,0:T(8,128)S(1)} copy(s32[512,1]{0,1:T(1,128)} %param.16) | data formatting | bytes 4096 | tf_op args[6]
  1.5 0.0 copy-start
  1.5 0.0 copy-start.1
  1.5 0.0 copy-start.2
  1.5 0.0 copy-start.3
  1.5 0.0 copy-start.4
  1.5 0.0 copy-start.5
  1.5 5.7 %copy.14.basis_hbm = f32[128,64,64]{2,1,0:T(8,128)} copy(f32[128,64,64]{0,2,1:T(8,128)} %param.19) | data formatting | bytes 4194304 | tf_op args[9]
  7.2 0.0 copy-done
  7.2 0.0 copy-done.1
  7.2 0.0 copy-done.2
  7.2 0.0 copy-done.3
  7.2 0.0 copy-done.4
  7.3 0.0 copy-done.5
  7.3 65.0 %shard_map.121 = (f32[3,64,32,128]{3,2,1,0:T(8,128)}, f32[3,64,32,128]{3,2,1,0:T(8,128)}, f32[1,128]{1,0:T(1,128)S(1)}) custom-call(s32[512,1]{1,0:T(8,128)S(1)} %copy.13.tile_col, s32[1,512]{1,0:T(1,128)S(1)} %bitcast.2, s32[1,512]{1,0:T(1,128)S(1)} %bitcast.3, f32[8]{0:T(128)S(1)} %copy-done.4, s32[16]{0:T(128)S(1)} %copy-done.5, ...), custom_call_target="tpu_custom_call" | custom-call | tf_op jit(solution)/shard_map/pallas_call | solution.py:543
  72.2 0.0 copy-start.6
  72.3 4.0 %copy.18 = f32[3,64,32,128]{3,2,1,0:T(8,128)} copy(f32[3,64,32,128]{3,2,1,0:T(8,128)} %get-tuple-element.6) | data formatting | bytes 6291456
  76.3 0.0 copy-done.6
  76.3 1.7 %copy.19 = f32[3,64,32,128]{3,2,1,0:T(8,128)} copy(f32[3,64,32,128]{3,2,1,0:T(8,128)S(1)} %copy-done.6) | data formatting | bytes 6291456
  77.9 0.5 copy.20
Async XLA Ops:
  1.5 5.8 %copy-start = (s32[64,32,128]{2,1,0:T(8,128)S(1)}, s32[64,32,128]{2,1,0:T(8,128)}, u32[]{:S(2)}) copy-start(s32[64,32,128]{2,1,0:T(8,128)} %ids_hbm.1) | copy-start | bytes 3145732
  1.5 5.8 %copy-start.1 = (f32[512,384]{1,0:T(8,128)S(1)}, f32[512,384]{1,0:T(8,128)}, u32[]{:S(2)}) copy-start(f32[512,384]{1,0:T(8,128)} %values_hbm.1) | copy-start | bytes 2359300
  1.5 5.8 %copy-start.2 = (s32[512,1]{0,1:T(1,128)S(1)}, s32[512,1]{0,1:T(1,128)}, u32[]{:S(2)}) copy-start(s32[512,1]{0,1:T(1,128)} %param.16) | copy-start | bytes 6148
  1.5 5.7 %copy-start.3 = (s32[512]{0:T(512)S(1)}, s32[512]{0:T(512)}, u32[]{:S(2)}) copy-start(s32[512]{0:T(512)} %param.17) | copy-start | bytes 6148
  1.5 5.7 %copy-start.4 = (f32[8]{0:T(128)S(1)}, f32[8]{0:T(128)}, u32[]{:S(2)}) copy-start(f32[8]{0:T(128)} %table.1) | copy-start | bytes 100
  1.5 5.7 %copy-start.5 = (s32[16]{0:T(128)S(1)}, s32[16]{0:T(128)}, u32[]{:S(2)}) copy-start(s32[16]{0:T(128)} %owners.1) | copy-start | bytes 196
  72.2 4.0 %copy-start.6 = (f32[3,64,32,128]{3,2,1,0:T(8,128)S(1)}, f32[3,64,32,128]{3,2,1,0:T(8,128)}, u32[]{:S(2)}) copy-start(f32[3,64,32,128]{3,2,1,0:T(8,128)} %get-tuple-element.7) | copy-start | bytes 9437188
where the time goes:
time: 78.6 us; the launch traced here: 78.5 us
  Pallas kernels  65 us (83%)
  local copies, waits for them, and re-layouts  12.8 us (16%)
    pallas_call x1, Pallas kernels, per_device(): pl.pallas_call(functools.partial(kernel, grid_x, grid_y), out_shape=(jax....  65 us
    unnamed x19, local copies, waits for them, and re-layouts  12.8 us

commit v1 on v0

--- a/solution.py
+++ b/solution.py
@@ -22,7 +22,6 @@
 def kernel(
     grid_x,
     grid_y,
-    tile_col,
     tile_row,
     cell_row,
     table,
@@ -82,23 +81,33 @@
     index_y = lax.axis_index("gy")
     me = index_x * grid_y + index_y
 
-    def place(device):
-        return (device // grid_y, lax.rem(device, grid_y))
-
-    def others(body):
-        def step(k, carry):
-            body(lax.rem(me + k, n))
+    def others(body, first=0, last=grid_x):
+        def one(kx, ky):
+            x, y = index_x + kx, index_y + ky
+            x = jnp.where(x >= grid_x, x - grid_x, x)
+            y = jnp.where(y >= grid_y, y - grid_y, y)
+            body(x * grid_y + y, (x, y))
+
+        if first == 0:
+            for ky in range(1, grid_y):
+                one(0, ky)
+
+        def step(kx, carry):
+            for ky in range(grid_y):
+                one(kx, ky)
             return carry
 
-        lax.fori_loop(1, n, step, 0)
+        lax.fori_loop(max(first, 1), last, step, 0)
 
     barrier = pltpu.get_barrier_semaphore()
 
-    def greet(device):
-        pl.semaphore_signal(barrier, inc=1, device_id=place(device), device_id_type=MESH)
+    def greet(device, where):
+        pl.semaphore_signal(barrier, inc=1, device_id=where, device_id_type=MESH)
 
     others(greet)
 
+    side = basis_hbm.shape[0]
+    offset = pl.multiple_of(lax.rem(index_y * width_y, side), width_y)
     e_own = e.at[:, pl.ds(0, width_x)]
     h_own = h.at[:, pl.ds(1, width_x)]
     loads = [
@@ -110,7 +119,7 @@
                 (magnetic_hbm, h_own),
                 (ids_hbm, ids),
                 (forward_hbm, forward),
-                (basis_hbm, basis),
+                (basis_hbm.at[:, pl.ds(offset, width_y)], basis),
             ]
         )
     ]
@@ -118,11 +127,16 @@
         load.start()
 
     trow = tile_row[...]
-    same = (tile_col[...] == trow) & (
-        lax.broadcasted_iota(jnp.int32, (count, count), 0)
-        < lax.broadcasted_iota(jnp.int32, (count, count), 1)
+    to_tile = lax.broadcasted_iota(jnp.int32, (n, count), 0) == trow
+    earlier = lax.broadcasted_iota(jnp.int32, (count, count), 0) < (
+        lax.broadcasted_iota(jnp.int32, (count, count), 1)
     )
-    slot = jnp.sum(jnp.where(same, 1.0, 0.0), axis=0, keepdims=True).astype(jnp.int32)
+    before = jnp.dot(
+        jnp.where(to_tile, 1.0, 0.0).astype(jnp.bfloat16),
+        jnp.where(earlier, 1.0, 0.0).astype(jnp.bfloat16),
+        preferred_element_type=jnp.float32,
+    )
+    slot = jnp.sum(jnp.where(to_tile, before, 0.0), axis=0, keepdims=True).astype(jnp.int32)
     dest = trow * cap + slot
     chunk = min(256, rows)
 
@@ -167,33 +181,33 @@
         mine = pl.ds(pl.multiple_of(me * cap, cap), cap)
         got[step, mine, :] = packed[step, mine, :]
 
-    def send_values(step):
+    def send_values(step, first=0, last=grid_x):
         mine = pl.ds(pl.multiple_of(me * cap, cap), cap)
 
-        def send(device):
+        def send(device, where):
             pltpu.make_async_remote_copy(
                 src_ref=packed.at[step, pl.ds(pl.multiple_of(device * cap, cap), cap)],
                 dst_ref=got.at[step, mine],
                 send_sem=bulk_send.at[step],
                 recv_sem=bulk_recv.at[step],
-                device_id=place(device),
+                device_id=where,
                 device_id_type=MESH,
             ).start()
 
-        others(send)
+        others(send, first, last)
 
     def wait_values(step, sem):
         part = got.at[step, pl.ds(0, (n - 1) * cap)]
         pltpu.make_async_copy(part, part, sem.at[step]).wait()
 
     def send_blocks(source, target, number):
-        def send(device):
+        def send(device, where):
             pltpu.make_async_remote_copy(
                 src_ref=source(device),
                 dst_ref=target.at[me],
                 send_sem=bulk_send.at[number],
                 recv_sem=bulk_recv.at[number],
-                device_id=place(device),
+                device_id=where,
                 device_id_type=MESH,
             ).start()
 
@@ -285,10 +299,9 @@
     halo_start(1, 0)
     send_blocks(lambda device: cells_out.at[device], cells_got, steps)
     send_values(0)
-    for step in range(1, steps):
+    for step in range(1, min(steps, 2)):
         pack(step)
 
-    loads[3].wait()
     scalars = [time_step * table[m] for m in range(table.shape[0])]
 
     def fill_eps(i, carry):
@@ -300,8 +313,6 @@
         half_eps[part] = value
         acc[part] = jnp.zeros(which.shape, jnp.float32)
         return carry
-
-    lax.fori_loop(0, width_x // PLANES, fill_eps, 0)
 
     plane = (width_y, depth)
     row_id = lax.broadcasted_iota(jnp.int32, plane, 0)
@@ -358,7 +369,9 @@
         halo_start(2, step)
         halo_start(3, step)
 
-    def e_phase(step, first, last):
+    def e_phase(step, first, last, carry_in):
+        final = step + 1 == steps
+
         def body(i, carry):
             done = []
             for k in range(PLANES):
@@ -385,15 +398,19 @@
                 e[0, x] = ex
                 e[1, x] = ey
                 e[2, x] = ez
-                acc[x] = total
-                if step + 1 < steps:
+                if final:
+                    part = jnp.sum(total, axis=1, keepdims=True) * basis[x]
+                    for y in range(0, width_y, 8):
+                        carry = carry + part[y : y + 8]
+                else:
+                    acc[x] = total
                     ey_out[step + 1, 0, pl.ds(x, 1), :] = ex[:1, :]
                     ey_out[step + 1, 1, pl.ds(x, 1), :] = ez[:1, :]
             return carry
 
-        lax.fori_loop(first // PLANES, last // PLANES, body, 0)
-
-    tile_rows = min(256, cell_total)
+        return lax.fori_loop(first // PLANES, last // PLANES, body, carry_in)
+
+    tile_rows = min(512, cell_total)
 
     def make_drive(step):
         high, low = split_bf16(got[step])
@@ -419,11 +436,17 @@
     for step in range(steps):
         h_phase(step)
         if step == 0:
+            if steps > 1:
+                send_values(1)
+            for later in range(2, steps):
+                pack(later)
+            loads[3].wait()
+            lax.fori_loop(0, width_x // PLANES, fill_eps, 0)
             loads[4].wait()
             loads[5].wait()
-        if step + 1 < steps:
-            send_values(step + 1)
-        else:
+        elif step + 1 < steps:
+            send_values(step + 1, grid_x // 2, grid_x)
+        if step + 1 == steps:
             store = pltpu.make_async_copy(h_own, magnetic_out, store_sem.at[0])
             store.start()
             stores.append(store)
@@ -453,15 +476,18 @@
         h[1:3, 0] = h_store_plane
         halo_arrived(3, step)
         if step + 1 < steps:
-            e_phase(step, 0, width_x)
+            e_phase(step, 0, width_x, 0)
             ex_out[step + 1] = e[1:3, 0]
             halo_start(0, step + 1)
             halo_start(1, step + 1)
+            if step + 2 < steps:
+                send_values(step + 2, 0, grid_x // 2)
         else:
+            grad = jnp.zeros(grad_send.shape, jnp.float32)
             parts = 4
             size = width_x // parts
             for part in range(parts):
-                e_phase(step, part * size, (part + 1) * size)
+                grad = e_phase(step, part * size, (part + 1) * size, grad)
                 store = pltpu.make_async_copy(
                     e.at[:, pl.ds(part * size, size)],
                     electric_out.at[:, pl.ds(part * size, size)],
@@ -470,27 +496,7 @@
                 store.start()
                 stores.append(store)
 
-    side = basis.shape[1]
-    offset = lax.rem(index_y * width_y, side)
-    at_lane = lax.broadcasted_iota(jnp.int32, (width_y, side), 1) == (
-        lax.broadcasted_iota(jnp.int32, (width_y, side), 0) + offset
-    )
-    column = jnp.sum(acc[...], axis=2, keepdims=True) * corr_scale
-    corr = jnp.sum(jnp.where(at_lane[None], column, 0.0), axis=1)
-    params = basis.shape[0]
-    group = 16
-    pieces = []
-    ones = jnp.ones((8, side), jnp.float32)
-    for start in range(0, params, group):
-        pieces.append(jnp.sum(basis[start : start + group] * corr[None], axis=1))
-    weighted = jnp.concatenate(pieces, axis=0)
-    grad_send[...] = lax.dot_general(
-        ones,
-        weighted,
-        (((1,), (1,)), ((), ())),
-        preferred_element_type=jnp.float32,
-        precision=lax.Precision.HIGHEST,
-    )
+    grad_send[...] = grad * corr_scale
     grad_got[me] = grad_send[...]
     send_blocks(lambda device: grad_send, grad_got, steps + 1)
     wait_blocks(grad_got, bulk_recv, steps + 1)
@@ -501,7 +507,7 @@
         return total + jnp.where(owners[block] == me, grad_got[source], 0.0)
 
     total = lax.fori_loop(0, n, add, jnp.zeros(grad_send.shape, jnp.float32))
-    grad_out[...] = total[:1, :]
+    grad_out[...] = jnp.sum(total, axis=0, keepdims=True)
 
     for store in stores:
         store.wait()
@@ -511,6 +517,23 @@
             halo_left(which, step)
     wait_blocks(cells_got, bulk_send, steps)
     wait_blocks(grad_got, bulk_send, steps + 1)
+
+
+def hand_over(electric, magnetic, grad, electric_out, magnetic_out, grad_out, sem):
+    size = electric.shape[1] // 4
+    copies = []
+    for i, (source, dest) in enumerate([(electric, electric_out), (magnetic, magnetic_out)]):
+        for c in range(3):
+            for k in range(4):
+                part = pl.ds(k * size, size)
+                copies.append(
+                    pltpu.make_async_copy(source.at[c, part], dest.at[c, part], sem.at[i, c, k])
+                )
+    for copy in copies:
+        copy.start()
+    grad_out[...] = grad[...]
+    for copy in copies:
+        copy.wait()
 
 
 def per_device(
@@ -540,14 +563,14 @@
     hbm = pl.BlockSpec(memory_space=pl.ANY)
     x_face = pltpu.VMEM((steps, 2, width_y, depth), f32)
     y_face = pltpu.VMEM((steps, 2, width_x, depth), f32)
-    return pl.pallas_call(
+    results = pl.pallas_call(
         functools.partial(kernel, grid_x, grid_y),
         out_shape=(
             jax.ShapeDtypeStruct(electric.shape, f32),
             jax.ShapeDtypeStruct(magnetic.shape, f32),
             jax.ShapeDtypeStruct((1, params), f32),
         ),
-        in_specs=[vmem, vmem, vmem, smem, smem] + [hbm] * 6,
+        in_specs=[vmem, vmem, smem, smem] + [hbm] * 6,
         out_specs=(hbm, hbm, vmem),
         scratch_shapes=[
             pltpu.VMEM(source_values.shape, f32),
@@ -555,7 +578,7 @@
             pltpu.VMEM((3, width_x + 1, width_y, depth), f32),
             pltpu.VMEM(material_ids.shape, jnp.int32),
             pltpu.VMEM(forward_field.shape, bf16),
-            pltpu.VMEM(shape_basis.shape, f32),
+            pltpu.VMEM((width_x, width_y, params), f32),
             pltpu.VMEM(material_ids.shape, f32),
             pltpu.VMEM(material_ids.shape, f32),
             pltpu.VMEM(material_ids.shape, f32),
@@ -585,10 +608,9 @@
             pltpu.SemaphoreType.DMA((4, steps)),
         ],
         compiler_params=pltpu.CompilerParams(
-            collective_id=0, has_side_effects=True, vmem_limit_bytes=50 * 1024 * 1024
+            collective_id=0, has_side_effects=True, vmem_limit_bytes=60 * 1024 * 1024
         ),
     )(
-        source_tile,
         source_tile.reshape(1, count),
         source_cell.reshape(1, count),
         inv_permittivity,
@@ -598,8 +620,16 @@
         magnetic,
         material_ids,
         forward_field,
-        shape_basis,
+        jnp.transpose(shape_basis, (1, 2, 0)),
     )
+    return pl.pallas_call(
+        hand_over,
+        out_shape=tuple(jax.ShapeDtypeStruct(r.shape, r.dtype) for r in results),
+        in_specs=[hbm, hbm, vmem],
+        out_specs=(hbm, hbm, vmem),
+        scratch_shapes=[pltpu.SemaphoreType.DMA((2, 3, 4))],
+        compiler_params=pltpu.CompilerParams(vmem_limit_bytes=60 * 1024 * 1024),
+    )(*results)
 
 
 def solution(mesh):

time: 78.6 us -> 259 us (3.30)
  Pallas kernels: 65 us -> 258 us
  local copies, waits for them, and re-layouts: 12.8 us -> 0 us
    pallas_call x0 -> x1, Pallas kernels: none -> 193 us  [per_device(): pl.pallas_call(hand_over, out_shape=tuple((jax.ShapeDtypeStruct(r.shape,...]
    unnamed x19 -> x0, local copies, waits for them, and re-layouts: 12.8 us -> none
where the time goes in v1:
time: 259 us
  Pallas kernels  258 us (100%)
    pallas_call x1, Pallas kernels, per_device(): pl.pallas_call(hand_over, out_shape=tuple((jax.ShapeDtypeStruct(r.shape,...  193 us
    pallas_call x1, Pallas kernels, per_device(): pl.pallas_call(functools.partial(kernel, grid_x, grid_y), out_shape=(jax....  65.2 us

profile of v1, /device:TPU:0, one launch (start us, length us, event | category | flops | bytes accessed | tf_op | source)
XLA Modules:
  0.0 258.9 jit_solution(549030508753608797)
XLA Ops:
  0.6 65.2 %shard_map.121 = (f32[3,64,32,128]{3,2,1,0:T(8,128)}, f32[3,64,32,128]{3,2,1,0:T(8,128)}, f32[1,128]{1,0:T(1,128)}) custom-call(s32[1,512]{1,0:T(1,128)} %bitcast.4, s32[1,512]{1,0:T(1,128)} %bitcast.5, f32[8]{0:T(128)} %table.1, s32[16]{0:T(128)} %owners.1, f32[512,384]{1,0:T(8,128)} %values_hbm.1, f32[3,64,32,128]{3,2,1,0:T(8,128)} %electric_hbm.1, ...), custom_call_target="tpu_custom_call" | custom-call | tf_op jit(solution)/shard_map/pallas_call | solution.py:566
  65.9 193.0 %shard_map.122 = (f32[3,64,32,128]{3,2,1,0:T(8,128)}, f32[3,64,32,128]{3,2,1,0:T(8,128)}, f32[1,128]{1,0:T(1,128)}) custom-call(f32[3,64,32,128]{3,2,1,0:T(8,128)} %get-tuple-element.6.electric, f32[3,64,32,128]{3,2,1,0:T(8,128)} %get-tuple-element.7.magnetic, f32[1,128]{1,0:T(1,128)} %get-tuple-element.8.grad), custom_call_target="tpu_custom_call" | custom-call | tf_op jit(solution)/shard_map/pallas_call | solution.py:625

commit v2 on v1

--- a/solution.py
+++ b/solution.py
@@ -88,16 +88,16 @@
             y = jnp.where(y >= grid_y, y - grid_y, y)
             body(x * grid_y + y, (x, y))
 
-        if first == 0:
-            for ky in range(1, grid_y):
-                one(0, ky)
-
-        def step(kx, carry):
+        def step(i, carry):
+            kx = grid_x // 2 + (2 * lax.rem(i, 2) - 1) * ((i + 1) // 2)
             for ky in range(grid_y):
                 one(kx, ky)
             return carry
 
-        lax.fori_loop(max(first, 1), last, step, 0)
+        lax.fori_loop(first, min(last, grid_x - 1), step, 0)
+        if last == grid_x:
+            for ky in range(1, grid_y):
+                one(0, ky)
 
     barrier = pltpu.get_barrier_semaphore()
 
@@ -519,21 +519,34 @@
     wait_blocks(grad_got, bulk_send, steps + 1)
 
 
-def hand_over(electric, magnetic, grad, electric_out, magnetic_out, grad_out, sem):
+def hand_over(
+    electric, magnetic, grad, electric_out, magnetic_out, grad_out, held_e, held_h, in_sem, out_sem
+):
     size = electric.shape[1] // 4
     copies = []
-    for i, (source, dest) in enumerate([(electric, electric_out), (magnetic, magnetic_out)]):
+    arrays = [(electric, held_e, electric_out), (magnetic, held_h, magnetic_out)]
+    for i, (source, held, dest) in enumerate(arrays):
         for c in range(3):
             for k in range(4):
                 part = pl.ds(k * size, size)
                 copies.append(
-                    pltpu.make_async_copy(source.at[c, part], dest.at[c, part], sem.at[i, c, k])
+                    (
+                        pltpu.make_async_copy(
+                            source.at[c, part], held.at[c, part], in_sem.at[i, c, k]
+                        ),
+                        pltpu.make_async_copy(
+                            held.at[c, part], dest.at[c, part], out_sem.at[i, c, k]
+                        ),
+                    )
                 )
-    for copy in copies:
-        copy.start()
+    for load, _ in copies:
+        load.start()
     grad_out[...] = grad[...]
-    for copy in copies:
-        copy.wait()
+    for load, store in copies:
+        load.wait()
+        store.start()
+    for _, store in copies:
+        store.wait()
 
 
 def per_device(
@@ -627,7 +640,12 @@
         out_shape=tuple(jax.ShapeDtypeStruct(r.shape, r.dtype) for r in results),
         in_specs=[hbm, hbm, vmem],
         out_specs=(hbm, hbm, vmem),
-        scratch_shapes=[pltpu.SemaphoreType.DMA((2, 3, 4))],
+        scratch_shapes=[
+            pltpu.VMEM(electric.shape, f32),
+            pltpu.VMEM(magnetic.shape, f32),
+            pltpu.SemaphoreType.DMA((2, 3, 4)),
+            pltpu.SemaphoreType.DMA((2, 3, 4)),
+        ],
         compiler_params=pltpu.CompilerParams(vmem_limit_bytes=60 * 1024 * 1024),
     )(*results)
 

time: 259 us -> 72.7 us (0.28)
  Pallas kernels: 258 us -> 71.9 us
    pallas_call x1, Pallas kernels: 193 us -> 6.7 us  [per_device(): pl.pallas_call(hand_over, out_shape=tuple((jax.ShapeDtypeStruct(r.shape,...]
where the time goes in v2:
time: 72.7 us; the launch traced here: 72.6 us
  Pallas kernels  71.9 us (99%)
    pallas_call x1, Pallas kernels, per_device(): pl.pallas_call(functools.partial(kernel, grid_x, grid_y), out_shape=(jax....  65.2 us
    pallas_call x1, Pallas kernels, per_device(): pl.pallas_call(hand_over, out_shape=tuple((jax.ShapeDtypeStruct(r.shape,...  6.7 us

profile of v2, /device:TPU:0, one launch (start us, length us, event | category | flops | bytes accessed | tf_op | source)
XLA Modules:
  0.0 72.6 jit_solution(1484811429160490998)
XLA Ops:
  0.6 65.2 %shard_map.121 = (f32[3,64,32,128]{3,2,1,0:T(8,128)}, f32[3,64,32,128]{3,2,1,0:T(8,128)}, f32[1,128]{1,0:T(1,128)}) custom-call(s32[1,512]{1,0:T(1,128)} %bitcast.4, s32[1,512]{1,0:T(1,128)} %bitcast.5, f32[8]{0:T(128)} %table.1, s32[16]{0:T(128)} %owners.1, f32[512,384]{1,0:T(8,128)} %values_hbm.1, f32[3,64,32,128]{3,2,1,0:T(8,128)} %electric_hbm.1, ...), custom_call_target="tpu_custom_call" | custom-call | tf_op jit(solution)/shard_map/pallas_call | solution.py:579
  65.9 6.7 %shard_map.122 = (f32[3,64,32,128]{3,2,1,0:T(8,128)}, f32[3,64,32,128]{3,2,1,0:T(8,128)}, f32[1,128]{1,0:T(1,128)}) custom-call(f32[3,64,32,128]{3,2,1,0:T(8,128)} %get-tuple-element.6.electric, f32[3,64,32,128]{3,2,1,0:T(8,128)} %get-tuple-element.7.magnetic, f32[1,128]{1,0:T(1,128)} %get-tuple-element.8.grad), custom_call_target="tpu_custom_call" | custom-call | tf_op jit(solution)/shard_map/pallas_call | solution.py:638
